TPU v7x, 32 devices: a whole 2x2x4 slice. The times are simulated.
32 devices in a mesh: dp: 2 (over core), seq: 16 (over z, y, x).
Axes of the slice: x: 2, y: 2, z: 4, core: 2. Of those that a mesh axis runs over, the one named last changes fastest.
Arguments:
- queries: bfloat16 [2, 2048, 2048], P('dp', 'seq'), may hold values from -62 to 62
- keys: bfloat16 [2, 2048, 2048], P('dp', 'seq'), may hold values from -4 to 4
- values: bfloat16 [2, 2048, 2048], P('dp', 'seq'), may hold values from -4 to 4
- cotangent: bfloat16 [2, 2048, 2048], P('dp', 'seq'), may hold values from -4 to 4
- cluster_of: int32 [2, 16, 32], P('dp', None, 'seq'), may hold values from 0 to 127, as said below
- block_list: int32 [2, 2048, 4], P('dp', 'seq'), may hold values from -1 to 31, as said below
- centroid_sums: float32 [2048, 128], P('seq'), may hold values from -5 to 5
Outputs:
- attn_out: bfloat16 [2, 2048, 2048], P('dp', 'seq')
- grad_q: bfloat16 [2, 2048, 2048], P('dp', 'seq')
- grad_k: bfloat16 [2, 2048, 2048], P('dp', 'seq')
- grad_v: bfloat16 [2, 2048, 2048], P('dp', 'seq')
- centroid_next: float32 [2048, 128], P('seq')
Inputs may be any that keep to these rules, and one draw needn't show every extreme that they name: cluster_of[d, h, b] is the cluster under head h of block b of document d; the centroid of cluster c of head h lies on seq index h + c // 128. Of the 2 blocks on one seq index, at most 2 share the value c // 128 under one head, and in every draw some reach 2. Row h * 128 + c of block_list[d] lists in increasing order the blocks b with cluster_of[d, h, b] == c, then -1; every block appears once for each head; a cluster holds at most 4 blocks, and in every draw some cluster holds exactly 4.
All inputs are finite; a program needn't handle non-finite values.
Results may differ from a plain program's by a relative error of at most 0.015.
Values may be sent and summed in bfloat16 or wider, within the bound.
A program may use at most 128 MiB of HBM per device.

v0:
```python
import math

import jax
import jax.numpy as jnp
from jax import lax
from jax.sharding import PartitionSpec as P

decay_rate = 0.99
neg_fill = -1e30


def shortened(x):
    return jax.tree.map(lambda a: a.astype(jnp.bfloat16) if a.dtype == jnp.float32 else a, x)


def forward_tiles(q_tiles, k_tiles, v_tiles, positions, present_rows):
    score_scale = 1.0 / math.sqrt(q_tiles.shape[-1])
    scores = (
        jnp.einsum("crd,csd->crs", q_tiles, k_tiles, preferred_element_type=jnp.float32)
        * score_scale
    )
    visible = present_rows[:, :, None] & present_rows[:, None, :]
    visible = visible & (positions[:, None, :] <= positions[:, :, None])
    scores = jnp.where(visible, scores, neg_fill)
    row_max = jnp.max(scores, axis=-1, keepdims=True)
    raised = jnp.exp(scores - row_max)
    probabilities = jnp.where(visible, raised / jnp.sum(raised, axis=-1, keepdims=True), 0.0)
    weights = probabilities.astype(jnp.bfloat16)
    out_full = jnp.einsum("crs,csd->crd", weights, v_tiles, preferred_element_type=jnp.float32)
    return (probabilities, weights, out_full, score_scale)


def output_tiles(q_tiles, k_tiles, v_tiles, positions, present_rows):
    results = forward_tiles(q_tiles, k_tiles, v_tiles, positions, present_rows)
    return (results[2].astype(jnp.bfloat16),)


def all_tiles(q_tiles, k_tiles, v_tiles, d_tiles, positions, present_rows):
    probabilities, weights, out_full, score_scale = forward_tiles(
        q_tiles, k_tiles, v_tiles, positions, present_rows
    )
    dprobs = jnp.einsum("crd,csd->crs", d_tiles, v_tiles, preferred_element_type=jnp.float32)
    row_dot = jnp.sum(d_tiles.astype(jnp.float32) * out_full, axis=-1, keepdims=True)
    dscores = (probabilities * (dprobs - row_dot) * score_scale).astype(jnp.bfloat16)
    grad_values = jnp.einsum("crs,crd->csd", weights, d_tiles, preferred_element_type=jnp.float32)
    grad_queries = jnp.einsum("crs,csd->crd", dscores, k_tiles, preferred_element_type=jnp.float32)
    grad_keys = jnp.einsum("crs,crd->csd", dscores, q_tiles, preferred_element_type=jnp.float32)
    return (
        out_full.astype(jnp.bfloat16),
        grad_queries.astype(jnp.bfloat16),
        grad_keys.astype(jnp.bfloat16),
        grad_values.astype(jnp.bfloat16),
    )


def grad_tiles(q_tiles, k_tiles, v_tiles, d_tiles, positions, present_rows):
    return all_tiles(q_tiles, k_tiles, v_tiles, d_tiles, positions, present_rows)[1:]


def per_device(queries, keys, values, cotangent, cluster_of, block_list, centroid_sums):
    seq_size = lax.axis_size("seq")
    head_count = cluster_of.shape[1]
    block_count = cluster_of.shape[2]
    token_count = queries.shape[1]
    block_len = token_count // block_count
    head_dim = centroid_sums.shape[1]
    groups_here = block_list.shape[1]
    cluster_cap = block_list.shape[2]
    owner_count = seq_size // head_count
    slot_cap = min(block_count, max(1, 2 * block_count // owner_count))
    tile_rows = cluster_cap * block_len
    step_target = 1 << max(0, max(1, 2048 // tile_rows).bit_length() - 1)
    group_size = math.gcd(groups_here, step_target)
    cluster_ids = cluster_of[0]
    owner_local = cluster_ids // groups_here
    earlier = jnp.arange(block_count)[:, None] < jnp.arange(block_count)[None, :]
    same_owner = owner_local[:, :, None] == owner_local[:, None, :]
    slot_of = jnp.sum(same_owner & earlier[None], axis=1)
    selector = owner_local[:, None, None, :] == jnp.arange(owner_count)[None, :, None, None]
    selector = selector & (slot_of[:, None, None, :] == jnp.arange(slot_cap)[None, None, :, None])
    selector = selector.astype(jnp.bfloat16)

    def pack(source):
        blocks_in = source[0].reshape(block_count, block_len, head_count, head_dim)
        outgoing = jnp.einsum(
            "hlcj,jthd->hlctd", selector, blocks_in, preferred_element_type=jnp.float32
        )
        return outgoing.astype(jnp.bfloat16).reshape(seq_size, slot_cap, block_len, head_dim)

    def unpack(returned):
        arranged = returned.reshape(head_count, owner_count, slot_cap, block_len, head_dim)
        gathered = jnp.einsum(
            "hlcj,hlctd->jthd", selector, arranged, preferred_element_type=jnp.float32
        )
        return gathered.astype(jnp.bfloat16).reshape(1, token_count, head_count * head_dim)

    members = block_list[0].reshape(-1)
    present = members >= 0
    source_dev = jnp.where(present, members // block_count, -1)
    before = (
        present[None, :]
        & (source_dev[None, :] == source_dev[:, None])
        & (members[None, :] < members[:, None])
    )
    slot_at = jnp.sum(before, axis=1)
    recv_row = jnp.where(present, source_dev * slot_cap + slot_at, 0)
    drop_row = jnp.where(present, source_dev * slot_cap + slot_at, seq_size * slot_cap)
    token_offsets = jnp.arange(block_len)
    positions = (
        jnp.where(present, members, 0)[:, None] * block_len + token_offsets[None, :]
    ).reshape(groups_here, tile_rows)
    present_rows = jnp.broadcast_to(present[:, None], (members.shape[0], block_len)).reshape(
        groups_here, tile_rows
    )

    def to_tiles(arrived):
        flat_rows = arrived.reshape(seq_size * slot_cap, block_len, head_dim)
        return flat_rows[recv_row].reshape(groups_here, tile_rows, head_dim)

    def from_tiles(tiles_in):
        flat_rows = jnp.zeros((seq_size * slot_cap, block_len, head_dim), jnp.bfloat16)
        flat_rows = flat_rows.at[drop_row].set(
            tiles_in.reshape(-1, block_len, head_dim), mode="drop"
        )
        return flat_rows.reshape(seq_size, slot_cap, block_len, head_dim)

    def grouped(worker, tiles_all):
        shaped = tuple(
            (
                item.reshape((groups_here // group_size, group_size) + item.shape[1:])
                for item in tiles_all
            )
        )
        outcome = lax.map(lambda tiles_in: worker(*tiles_in), shaped)
        return tuple((item.reshape((groups_here,) + item.shape[2:]) for item in outcome))

    arrived = (
        lax.all_to_all(pack(queries), "seq", split_axis=0, concat_axis=0, tiled=True),
        lax.all_to_all(pack(keys), "seq", split_axis=0, concat_axis=0, tiled=True),
        lax.all_to_all(pack(values), "seq", split_axis=0, concat_axis=0, tiled=True),
    )
    q_tiles, key_tiles, v_tiles = (to_tiles(item) for item in arrived)
    forward_out = grouped(output_tiles, (q_tiles, key_tiles, v_tiles, positions, present_rows))
    out_back = lax.all_to_all(
        from_tiles(forward_out[0]), "seq", split_axis=0, concat_axis=0, tiled=True
    )
    d_arrived = lax.all_to_all(pack(cotangent), "seq", split_axis=0, concat_axis=0, tiled=True)
    d_tiles = to_tiles(d_arrived)
    gradients = grouped(grad_tiles, (q_tiles, key_tiles, v_tiles, d_tiles, positions, present_rows))
    grads_back = lax.all_to_all(
        shortened(tuple((from_tiles(item) for item in gradients))),
        "seq",
        split_axis=0,
        concat_axis=0,
        tiled=True,
    )
    returned = (out_back,) + tuple(grads_back)
    key_sum = jnp.einsum(
        "cr,crd->cd",
        present_rows.astype(jnp.bfloat16),
        key_tiles,
        preferred_element_type=jnp.float32,
    )
    summed = lax.psum(key_sum, "dp")
    centroid_next = decay_rate * centroid_sums + (1.0 - decay_rate) * summed
    return (
        unpack(returned[0]),
        unpack(returned[1]),
        unpack(returned[2]),
        unpack(returned[3]),
        centroid_next,
    )


def solution(mesh):
    in_specs = (
        P("dp", "seq", None),
        P("dp", "seq", None),
        P("dp", "seq", None),
        P("dp", "seq", None),
        P("dp", None, "seq"),
        P("dp", "seq", None),
        P("seq", None),
    )
    out_specs = (
        P("dp", "seq", None),
        P("dp", "seq", None),
        P("dp", "seq", None),
        P("dp", "seq", None),
        P("seq", None),
    )
    return jax.shard_map(
        per_device, mesh=mesh, in_specs=in_specs, out_specs=out_specs, check_vma=False
    )
```

profile of v0, /device:TPU:0, one launch (start us, length us, event | category | flops | bytes accessed | tf_op | source)
XLA Modules:
  0.0 745.0 jit_solution(66589653398034807)
XLA Ops:
  11.4 8.3 %all-to-all-start.1 = ((bf16[16,2,64,128]{3,1,2,0:T(2,128)(2,1)}), bf16[16,2,64,128]{3,1,2,0:T(2,128)(2,1)S(1)}, u32[]{:S(2)}, u32[]{:S(2)}) async-start(bf16[16,2,64,128]{3,1,2,0:T(2,128)(2,1)} %convolution_convert_fusion.10), calls=%async_computation.1 | async-start | bytes 1048576 | tf_op jit(solution)/shard_map/all_to_all | solution.py:139
  22.9 11.9 %all-to-all-done.1 = bf16[16,2,64,128]{3,1,2,0:T(2,128)(2,1)S(1)} async-done(((bf16[16,2,64,128]{3,1,2,0:T(2,128)(2,1)}), bf16[16,2,64,128]{3,1,2,0:T(2,128)(2,1)S(1)}, u32[]{:S(2)}, u32[]{:S(2)}) %all-to-all-start.1) | async-done | bytes 524320 | tf_op jit(solution)/shard_map/all_to_all | solution.py:139
  41.0 12.3 %all-to-all-done = bf16[16,2,64,128]{3,1,2,0:T(2,128)(2,1)S(1)} async-done(((bf16[16,2,64,128]{3,1,2,0:T(2,128)(2,1)}), bf16[16,2,64,128]{3,1,2,0:T(2,128)(2,1)S(1)}, u32[]{:S(2)}, u32[]{:S(2)}) %all-to-all-start) | async-done | bytes 524320 | tf_op jit(solution)/shard_map/all_to_all | solution.py:138
  59.7 11.7 %all-to-all-done.2 = bf16[16,2,64,128]{3,1,2,0:T(2,128)(2,1)S(1)} async-done(((bf16[16,2,64,128]{3,1,2,0:T(2,128)(2,1)}), bf16[16,2,64,128]{3,1,2,0:T(2,128)(2,1)S(1)}, u32[]{:S(2)}, u32[]{:S(2)}) %all-to-all-start.2) | async-done | bytes 524320 | tf_op jit(solution)/shard_map/all_to_all | solution.py:140
  71.4 4.4 all-to-all-start.4
  77.7 13.0 %gather_fusion.1 = bf16[512,64,128]{2,1,0:T(8,128)(2,1)} fusion(bf16[32,64,128]{2,1,0:T(8,128)(2,1)S(1)} %bitcast.223, s32[1024]{0:T(1024)S(1)} %pad_clamp_fusion), kind=kCustom, calls=%fused_computation.1 | custom fusion | bytes 16779264 | tf_op jit(solution)/shard_map/gather | solution.py:118
  90.8 13.0 %gather_fusion = bf16[512,64,128]{2,1,0:T(8,128)(2,1)} fusion(bf16[32,64,128]{2,1,0:T(8,128)(2,1)S(1)} %bitcast.224, s32[1024]{0:T(1024)S(1)} %pad_clamp_fusion), kind=kCustom, calls=%fused_computation | custom fusion | bytes 16779264 | tf_op jit(solution)/shard_map/gather | solution.py:118
  103.9 13.2 %gather_fusion.2 = bf16[512,64,128]{2,1,0:T(8,128)(2,1)} fusion(bf16[32,64,128]{2,1,0:T(8,128)(2,1)S(1)} %bitcast.225, s32[1024]{0:T(1024)S(1)} %pad_clamp_fusion), kind=kCustom, calls=%fused_computation.2 | custom fusion | bytes 16779264 | tf_op jit(solution)/shard_map/gather | solution.py:118
  117.2 13.2 %gather_fusion.3 = bf16[512,64,128]{2,1,0:T(8,128)(2,1)} fusion(bf16[32,64,128]{2,1,0:T(8,128)(2,1)S(1)} %bitcast.222, s32[1024]{0:T(1024)S(1)} %pad_clamp_fusion), kind=kCustom, calls=%fused_computation.3 | custom fusion | bytes 16779264 | tf_op jit(solution)/shard_map/gather | solution.py:118
  130.4 5.3 broadcast.389.clone.1
  135.7 5.3 broadcast.389.clone.2
  141.0 5.3 broadcast.389.clone.3
  146.3 244.9 %while.25 = (s32[]{:T(128)}, bf16[16,8,256,128]{3,2,1,0:T(8,128)(2,1)}, bf16[16,8,256,128]{3,2,1,0:T(8,128)(2,1)}, bf16[16,8,256,128]{3,2,1,0:T(8,128)(2,1)}, pr...) while((s32[]{:T(128)}, ...), condition=%wide.region_11.12_spmd, body=%wide.region_7.11_spmd.sunk | while | flops 821557504 | bytes 17983604 | solution.py:134
  391.3 44.6 %scatter_fusion.1 = bf16[32,64,128]{2,1,0:T(8,128)(2,1)S(1)} fusion(bf16[32,64,128]{2,1,0:T(8,128)(2,1)S(1)} %broadcast.386.clone.1, s32[512]{0:T(512)S(1)} %bitcast.243, bf16[512,64,128]{2,1,0:T(8,128)(2,1)} %bitcast.36), kind=kCustom, calls=%fused_computation.5 | custom fusion | bytes 25167872 | tf_op jit(solution)/shard_map/scatter | solution.py:122
  437.2 7.0 all-to-all-start.5
  444.3 44.6 %scatter_fusion.2 = bf16[32,64,128]{2,1,0:T(8,128)(2,1)S(1)} fusion(bf16[32,64,128]{2,1,0:T(8,128)(2,1)S(1)} %broadcast.386.clone.2, s32[512]{0:T(512)S(1)} %bitcast.244, bf16[512,64,128]{2,1,0:T(8,128)(2,1)} %bitcast.40), kind=kCustom, calls=%fused_computation.6 | custom fusion | bytes 25167872 | tf_op jit(solution)/shard_map/scatter | solution.py:122
  490.3 6.9 all-to-all-start.6
  497.6 44.6 %scatter_fusion.3 = bf16[32,64,128]{2,1,0:T(8,128)(2,1)S(1)} fusion(bf16[32,64,128]{2,1,0:T(8,128)(2,1)S(1)} %broadcast.386.clone.3, s32[512]{0:T(512)S(1)} %bitcast.245, bf16[512,64,128]{2,1,0:T(8,128)(2,1)} %bitcast.228), kind=kCustom, calls=%fused_computation.7 | custom fusion | bytes 25167872 | tf_op jit(solution)/shard_map/scatter | solution.py:122
  543.6 5.2 fusion.97
  548.8 7.2 all-to-all-start.7
  556.0 5.3 broadcast.389.clone
  561.3 109.5 %while.24 = (s32[]{:T(128)}, bf16[16,8,256,128]{3,2,1,0:T(8,128)(2,1)}, pred[16,8,256]{2,1,0:T(8,128)(4,1)S(1)}, s32[16,8,256]{2,1,0:T(8,128)S(1)}, bf16[16,8,25...) while((s32[]{:T(128)}, ...), condition=%wide.region_5.6_spmd, body=%wide.region_2.5_spmd.sunk | while | flops 275513600 | bytes 6371421 | solution.py:134
  670.9 44.6 %scatter_fusion = bf16[32,64,128]{2,1,0:T(8,128)(2,1)S(1)} fusion(bf16[32,64,128]{2,1,0:T(8,128)(2,1)S(1)} %broadcast.386.clone, s32[512]{0:T(512)S(1)} %bitcast.246, bf16[512,64,128]{2,1,0:T(8,128)(2,1)} %bitcast.229), kind=kCustom, calls=%fused_computation.4 | custom fusion | bytes 25167872 | tf_op jit(solution)/shard_map/scatter | solution.py:122
  716.8 7.0 all-to-all-start.3
  (281 shorter events, 396.1 us)
Async XLA Ops:
  7.2 31.6 %copy-start = (bf16[1,128,2048]{2,1,0:T(8,128)(2,1)S(1)}, bf16[1,128,2048]{2,1,0:T(8,128)(2,1)}, u32[]{:S(2)}) copy-start(bf16[1,128,2048]{2,1,0:T(8,128)(2,1)} %param.13) | copy-start | bytes 1572868
  7.2 49.9 %copy-start.3 = (s32[1,128,4]{1,2,0:T(4,128)S(1)}, s32[1,128,4]{1,2,0:T(4,128)}, u32[]{:S(2)}) copy-start(s32[1,128,4]{1,2,0:T(4,128)} %param.16) | copy-start | bytes 6148
  7.2 50.2 %copy-start.1 = (bf16[1,128,2048]{2,1,0:T(8,128)(2,1)S(1)}, bf16[1,128,2048]{2,1,0:T(8,128)(2,1)}, u32[]{:S(2)}) copy-start(bf16[1,128,2048]{2,1,0:T(8,128)(2,1)} %param.14) | copy-start | bytes 1572868
  8.2 51.5 %copy-start.4 = (s32[16,2]{1,0:T(8,128)}, s32[16,2]{1,0:T(8,128)S(1)}, u32[]{:S(2)}) copy-start(s32[16,2]{1,0:T(8,128)S(1)} %copy.110) | copy-start | bytes 388
  8.3 51.4 %copy-start.6 = (pred[16,2]{1,0:T(8,128)(4,1)}, pred[16,2]{1,0:T(8,128)(4,1)S(1)}, u32[]{:S(2)}) copy-start(pred[16,2]{1,0:T(8,128)(4,1)S(1)} %copy.109) | copy-start | bytes 100
  11.4 23.5 %all-to-all-start.1 = ((bf16[16,2,64,128]{3,1,2,0:T(2,128)(2,1)}), bf16[16,2,64,128]{3,1,2,0:T(2,128)(2,1)S(1)}, u32[]{:S(2)}, u32[]{:S(2)}) async-start(bf16[16,2,64,128]{3,1,2,0:T(2,128)(2,1)} %convolution_convert_fusion.10), calls=%async_computation.1 | async-start | bytes 1048576 | tf_op jit(solution)/shard_map/all_to_all | solution.py:139
  34.9 18.3 %all-to-all-start = ((bf16[16,2,64,128]{3,1,2,0:T(2,128)(2,1)}), bf16[16,2,64,128]{3,1,2,0:T(2,128)(2,1)S(1)}, u32[]{:S(2)}, u32[]{:S(2)}) async-start(bf16[16,2,64,128]{3,1,2,0:T(2,128)(2,1)} %convolution_convert_fusion.11), calls=%async_computation | async-start | bytes 1048576 | tf_op jit(solution)/shard_map/all_to_all | solution.py:138
  53.2 18.2 %all-to-all-start.2 = ((bf16[16,2,64,128]{3,1,2,0:T(2,128)(2,1)}), bf16[16,2,64,128]{3,1,2,0:T(2,128)(2,1)S(1)}, u32[]{:S(2)}, u32[]{:S(2)}) async-start(bf16[16,2,64,128]{3,1,2,0:T(2,128)(2,1)} %convolution_convert_fusion.9), calls=%async_computation.2 | async-start | bytes 1048576 | tf_op jit(solution)/shard_map/all_to_all | solution.py:140
  71.4 45.7 %all-to-all-start.4 = ((bf16[16,2,64,128]{3,1,2,0:T(2,128)(2,1)}), bf16[16,2,64,128]{3,1,2,0:T(2,128)(2,1)S(1)}, u32[]{:S(2)}, u32[]{:S(2)}) async-start(bf16[16,2,64,128]{3,1,2,0:T(2,128)(2,1)} %convolution_convert_fusion.7), calls=%async_computation.4 | async-start | bytes 1048576 | tf_op jit(solution)/shard_map/all_to_all | solution.py:147
  437.2 53.0 %all-to-all-start.5 = ((bf16[16,2,64,128]{3,1,2,0:T(2,128)(2,1)}), bf16[16,2,64,128]{3,1,2,0:T(2,128)(2,1)S(1)}, u32[]{:S(2)}, u32[]{:S(2)}) async-start(bf16[16,2,64,128]{3,1,2,0:T(2,128)(2,1)} %copy.125), calls=%async_computation.5 | async-start | bytes 1048576 | tf_op jit(solution)/shard_map/all_to_all | solution.py:150
  490.3 58.5 %all-to-all-start.6 = ((bf16[16,2,64,128]{3,1,2,0:T(2,128)(2,1)}), bf16[16,2,64,128]{3,1,2,0:T(2,128)(2,1)S(1)}, u32[]{:S(2)}, u32[]{:S(2)}) async-start(bf16[16,2,64,128]{3,1,2,0:T(2,128)(2,1)} %copy.127), calls=%async_computation.6 | async-start | bytes 1048576 | tf_op jit(solution)/shard_map/all_to_all | solution.py:150
  497.2 226.7 %all-reduce.2.cloned.1.call-start = ((), (), s32[]{:S(2)}) async-start(), calls=%async_computation.8 | async-start | bytes 131072 | tf_op jit(solution)/shard_map/psum | solution.py:164
  548.8 168.0 %all-to-all-start.7 = ((bf16[16,2,64,128]{3,1,2,0:T(2,128)(2,1)}), bf16[16,2,64,128]{3,1,2,0:T(2,128)(2,1)S(1)}, u32[]{:S(2)}, u32[]{:S(2)}) async-start(bf16[16,2,64,128]{3,1,2,0:T(2,128)(2,1)} %copy.129), calls=%async_computation.7 | async-start | bytes 1048576 | tf_op jit(solution)/shard_map/all_to_all | solution.py:150
  670.9 53.0 %copy-start.2 = (f32[128,128]{1,0:T(8,128)S(1)}, f32[128,128]{1,0:T(8,128)}, u32[]{:S(2)}) copy-start(f32[128,128]{1,0:T(8,128)} %param.17) | copy-start | bytes 196612
  670.9 54.5 %copy-start.5 = (s32[16,2]{1,0:T(8,128)S(1)}, s32[16,2]{1,0:T(8,128)}, u32[]{:S(2)}) copy-start(s32[16,2]{1,0:T(8,128)} %copy-done.4) | copy-start | bytes 388
  670.9 54.5 %copy-start.7 = (pred[16,2]{1,0:T(8,128)(4,1)S(1)}, pred[16,2]{1,0:T(8,128)(4,1)}, u32[]{:S(2)}) copy-start(pred[16,2]{1,0:T(8,128)(4,1)} %copy-done.6) | copy-start | bytes 100
  716.8 18.9 %all-to-all-start.3 = ((bf16[16,2,64,128]{3,1,2,0:T(2,128)(2,1)}), bf16[16,2,64,128]{3,1,2,0:T(2,128)(2,1)S(1)}, u32[]{:S(2)}, u32[]{:S(2)}) async-start(bf16[16,2,64,128]{3,1,2,0:T(2,128)(2,1)} %copy.120), calls=%async_computation.3 | async-start | bytes 1048576 | tf_op jit(solution)/shard_map/all_to_all | solution.py:144
Sparse Core Ops, SparseCore 0:
  548.9 18.9 all-reduce.1
where the time goes:
time: 758 us; the launch traced here: 745 us
  matrix products  370 us (49%)
  local copies, waits for them, and re-layouts  268 us (35%)
  starting transfers between devices  48.6 us (6%)
  waiting for transfers between devices  39.9 us (5%)
  between operations  14.8 us (2%)
    scatter x4, local copies, waits for them, and re-layouts, from_tiles(): flat_rows.at[drop_row]  178 us
    sub x32, matrix products, forward_tiles(): raised = jnp.exp(scores - row_max)  101 us
    dot_general x32, matrix products, forward_tiles(): jnp.einsum('crs,csd->crd', weights, v_tiles, preferred_element_type=jnp.f...  100 us
    gather x4, local copies, waits for them, and re-layouts, to_tiles(): return flat_rows[recv_row].reshape(groups_here, tile_rows, head_dim)  52.3 us
    dot_general x16, matrix products, all_tiles(): jnp.einsum('crs,crd->csd', weights, d_tiles, preferred_element_type=jnp.f...  43.7 us
    dot_general x16, matrix products, all_tiles(): jnp.einsum('crs,csd->crd', dscores, k_tiles, preferred_element_type=jnp.f...  37.5 us
    dot_general x16, matrix products, all_tiles(): jnp.einsum('crs,crd->csd', dscores, q_tiles, preferred_element_type=jnp.f...  36.4 us
    dot_general x16, matrix products, all_tiles(): jnp.einsum('crd,csd->crs', d_tiles, v_tiles, preferred_element_type=jnp.f...  34.5 us
  transfers between devices with their start and end apart: 9, of which 4 were waited for; matrix products, arithmetic and copies ran while one was open for 42% of the time, Pallas kernels for 0%

commit v1 on v0

v1 whole, which is shorter than its diff:
```python
import functools
import math

import jax
import jax.numpy as jnp
from jax import lax
from jax.experimental import pallas as pl
from jax.experimental.pallas import tpu as pltpu
from jax.sharding import PartitionSpec as P

decay_rate = 0.99
neg_fill = -1e30
MESH = pl.DeviceIdType.MESH
PAIR = 2
NT = (((1,), (1,)), ((), ()))
TN = (((0,), (0,)), ((), ()))


def dot_f32(a, b, dims):
    return lax.dot_general(a, b, dims, preferred_element_type=jnp.float32)


def routed_kernel(
    seq_size, dp_size, slot_cap, block_len, head_dim, reach,
    order_ref, rank_ref, first_ref, slots_ref, cent_ref, k_ref, q_ref, v_ref, d_ref,
    out_ref, gq_ref, gk_ref, gv_ref, next_ref,
    k_in, q_in, v_in, d_in, ordered, acc_k, acc_v, made, back, key_rows, sums,
    in_send, in_recv, in_own, back_send, back_recv, back_own, sum_send, sum_recv,
):
    my_dp = lax.axis_index("dp")
    me = lax.axis_index("seq")
    slots = seq_size * slot_cap
    others = (seq_size - 1) * slot_cap
    lead = reach * block_len
    tile = PAIR * block_len
    window = lead + tile
    score_scale = 1.0 / math.sqrt(head_dim)

    barrier = pltpu.get_barrier_semaphore()

    def greet(step, carry):
        pl.semaphore_signal(
            barrier, inc=1, device_id=(my_dp, lax.rem(me + step, seq_size)), device_id_type=MESH
        )
        return carry

    lax.fori_loop(1, seq_size, greet, 0)
    for step in range(1, dp_size):
        pl.semaphore_signal(
            barrier, inc=1, device_id=(lax.rem(my_dp + step, dp_size), me), device_id_type=MESH
        )
    pl.semaphore_wait(barrier, seq_size + dp_size - 2)

    def columns(index):
        return pl.ds(pl.multiple_of(index * head_dim, head_dim), head_dim)

    def rows_of(index):
        return pl.ds(index * slot_cap, slot_cap)

    sources = (k_ref, q_ref, v_ref, d_ref)
    arrived = (k_in, q_in, v_in, d_in)
    for at, source in enumerate(sources):
        pltpu.make_async_copy(
            source.at[:, :, columns(me)], arrived[at].at[rows_of(me)], in_own.at[at]
        ).start()

        def send(step, carry, at=at, source=source):
            target = lax.rem(me + step, seq_size)
            pltpu.make_async_remote_copy(
                src_ref=source.at[:, :, columns(target)],
                dst_ref=arrived[at].at[rows_of(me)],
                send_sem=in_send.at[at],
                recv_sem=in_recv.at[at],
                device_id=(my_dp, target),
                device_id_type=MESH,
            ).start()
            return carry

        lax.fori_loop(1, seq_size, send, 0)

    ordered[:, :lead, :] = jnp.zeros((4, lead, head_dim), jnp.bfloat16)
    acc_k[...] = jnp.zeros_like(acc_k)
    acc_v[...] = jnp.zeros_like(acc_v)

    def bytes_of(at):
        return arrived[at].at[pl.ds(0, others)]

    for at, source in enumerate(sources):
        part = bytes_of(at)
        pltpu.make_async_copy(part, part, in_recv.at[at]).wait()
        pltpu.make_async_copy(
            source.at[:, :, columns(me)], arrived[at].at[rows_of(me)], in_own.at[at]
        ).wait()

        def place(spot, carry, at=at):
            rows = pl.ds(pl.multiple_of(lead + spot * block_len, block_len), block_len)
            ordered[at, rows, :] = arrived[at][order_ref[spot]]
            if at == 0:
                key_rows[pl.ds(spot, 1), :] = jnp.sum(
                    k_in[spot].astype(jnp.float32), axis=0, keepdims=True
                )
            return carry

        lax.fori_loop(0, slots, place, 0)
        if at == 0:
            groups = slots_ref.shape[0]
            spots = lax.broadcasted_iota(jnp.int32, (groups, slots), 1)
            member = jnp.zeros((groups, slots), jnp.float32)
            for one in range(slots_ref.shape[1]):
                member += jnp.where(slots_ref[:, one : one + 1] == spots, 1.0, 0.0)
            sums[my_dp] = lax.dot_general(
                member, key_rows[...], (((1,), (0,)), ((), ())),
                precision=lax.Precision.HIGHEST, preferred_element_type=jnp.float32,
            )
            for step in range(1, dp_size):
                target = lax.rem(my_dp + step, dp_size)
                pltpu.make_async_remote_copy(
                    src_ref=sums.at[my_dp],
                    dst_ref=sums.at[my_dp],
                    send_sem=sum_send.at[step],
                    recv_sem=sum_recv.at[step],
                    device_id=(target, me),
                    device_id_type=MESH,
                ).start()

    row_at = lax.broadcasted_iota(jnp.int32, (tile, window), 0)
    col_at = lax.broadcasted_iota(jnp.int32, (tile, window), 1)
    below = col_at <= row_at + lead
    row_one = lax.broadcasted_iota(jnp.int32, (tile, 1), 0)

    def attend(index, carry):
        start = pl.multiple_of(index * tile, tile)
        own = pl.ds(pl.multiple_of(start + lead, block_len), tile)
        near = pl.ds(start, window)
        k = ordered[0, near, :]
        q = ordered[1, own, :]
        v = ordered[2, near, :]
        g = ordered[3, own, :]
        low = jnp.zeros((tile, 1), jnp.int32)
        for one in range(PAIR):
            edge = lead + (first_ref[index * PAIR + one] - index * PAIR) * block_len
            low = jnp.where(row_one >= one * block_len, edge, low)
        visible = below & (col_at >= low)
        scores = jnp.where(visible, dot_f32(q, k, NT) * score_scale, neg_fill)
        raised = jnp.exp(scores - jnp.max(scores, axis=-1, keepdims=True))
        probs = raised / jnp.sum(raised, axis=-1, keepdims=True)
        weights = probs.astype(jnp.bfloat16)
        out_full = dot_f32(weights, v, (((1,), (0,)), ((), ())))
        dprobs = dot_f32(g, v, NT)
        row_dot = jnp.sum(g.astype(jnp.float32) * out_full, axis=-1, keepdims=True)
        dscores = (probs * (dprobs - row_dot) * score_scale).astype(jnp.bfloat16)
        here = pl.ds(index * PAIR, PAIR)
        tiled = (PAIR, block_len, head_dim)
        grad_q = dot_f32(dscores, k, (((1,), (0,)), ((), ())))
        made[0, here] = out_full.astype(jnp.bfloat16).reshape(tiled)
        made[1, here] = grad_q.astype(jnp.bfloat16).reshape(tiled)
        acc_k[near, :] += dot_f32(dscores, q, TN)
        acc_v[near, :] += dot_f32(weights, g, TN)
        return carry

    lax.fori_loop(0, slots // PAIR, attend, 0)
    made[2] = acc_k[lead:, :].astype(jnp.bfloat16).reshape(slots, block_len, head_dim)
    made[3] = acc_v[lead:, :].astype(jnp.bfloat16).reshape(slots, block_len, head_dim)

    results = (out_ref, gq_ref, gk_ref, gv_ref)
    for at, result in enumerate(results):

        def settle(spot, carry, at=at):
            back[at, spot] = made[at, rank_ref[spot]]
            return carry

        lax.fori_loop(0, slots, settle, 0)
        pltpu.make_async_copy(
            back.at[at, rows_of(me)], result.at[:, :, columns(me)], back_own.at[at]
        ).start()

        def give(step, carry, at=at, result=result):
            target = lax.rem(me + step, seq_size)
            pltpu.make_async_remote_copy(
                src_ref=back.at[at, rows_of(target)],
                dst_ref=result.at[:, :, columns(me)],
                send_sem=back_send.at[at],
                recv_sem=back_recv.at[at],
                device_id=(my_dp, target),
                device_id_type=MESH,
            ).start()
            return carry

        lax.fori_loop(1, seq_size, give, 0)

    for step in range(1, dp_size):
        source_dp = lax.rem(my_dp - step + dp_size, dp_size)
        swap = pltpu.make_async_remote_copy(
            src_ref=sums.at[my_dp],
            dst_ref=sums.at[source_dp],
            send_sem=sum_send.at[step],
            recv_sem=sum_recv.at[step],
            device_id=(lax.rem(my_dp + step, dp_size), me),
            device_id_type=MESH,
        )
        swap.wait_recv()
        swap.wait_send()
    total = sums[0]
    for one in range(1, dp_size):
        total = total + sums[one]
    next_ref[...] = decay_rate * cent_ref[...] + (1.0 - decay_rate) * total

    for at, result in enumerate(results):
        moved = bytes_of(at)
        pltpu.make_async_copy(moved, moved, in_send.at[at]).wait()
        pltpu.make_async_copy(moved, moved, back_recv.at[at]).wait()
        pltpu.make_async_copy(moved, moved, back_send.at[at]).wait()
        pltpu.make_async_copy(
            back.at[at, rows_of(me)], result.at[:, :, columns(me)], back_own.at[at]
        ).wait()


def per_device(queries, keys, values, cotangent, cluster_of, block_list, centroid_sums):
    seq_size = lax.axis_size("seq")
    dp_size = lax.axis_size("dp")
    head_count = cluster_of.shape[1]
    block_count = cluster_of.shape[2]
    token_count = queries.shape[1]
    block_len = token_count // block_count
    head_dim = centroid_sums.shape[1]
    groups_here = block_list.shape[1]
    cluster_cap = block_list.shape[2]
    owner_count = seq_size // head_count
    slot_cap = min(block_count, max(1, 2 * block_count // owner_count))
    slots = seq_size * slot_cap
    reach = -(-(cluster_cap - 1) // PAIR) * PAIR
    members = block_list[0]
    present = members >= 0
    if owner_count == 1:
        slot_table = members

        def pack(source):
            return source.reshape(block_count, block_len, seq_size * head_dim)

        def unpack(returned):
            return returned.reshape(1, token_count, head_count * head_dim)

    else:
        owner_local = cluster_of[0] // groups_here
        earlier = jnp.arange(block_count)[:, None] < jnp.arange(block_count)[None, :]
        same_owner = owner_local[:, :, None] == owner_local[:, None, :]
        slot_of = jnp.sum(same_owner & earlier[None], axis=1)
        selector = owner_local[:, None, None, :] == jnp.arange(owner_count)[None, :, None, None]
        selector = selector & (slot_of[:, None, None, :] == jnp.arange(slot_cap)[None, None, :, None])
        selector = selector.astype(jnp.bfloat16)

        def pack(source):
            blocks_in = source[0].reshape(block_count, block_len, head_count, head_dim)
            outgoing = jnp.einsum(
                "hlcj,jthd->cthld", selector, blocks_in, preferred_element_type=jnp.float32
            )
            return outgoing.astype(jnp.bfloat16).reshape(slot_cap, block_len, seq_size * head_dim)

        def unpack(returned):
            arranged = returned.reshape(slot_cap, block_len, head_count, owner_count, head_dim)
            gathered = jnp.einsum(
                "hlcj,cthld->jthd", selector, arranged, preferred_element_type=jnp.float32
            )
            return gathered.astype(jnp.bfloat16).reshape(1, token_count, head_count * head_dim)

        flat = members.reshape(-1)
        source_dev = jnp.where(flat >= 0, flat // block_count, -1)
        before = (
            (flat >= 0)[None, :]
            & (source_dev[None, :] == source_dev[:, None])
            & (flat[None, :] < flat[:, None])
        )
        slot_at = jnp.sum(before, axis=1)
        slot_table = jnp.where(flat >= 0, source_dev * slot_cap + slot_at, -1)
        slot_table = slot_table.reshape(members.shape).astype(jnp.int32)

    spots = jnp.arange(slots, dtype=jnp.int32)
    holds = slot_table.reshape(-1)[:, None] == spots[None, :]
    place = jnp.arange(holds.shape[0], dtype=jnp.int32)
    place_of = jnp.sum(jnp.where(holds, place[:, None] + 1, 0), axis=0)
    place_of = jnp.where(place_of > 0, place_of - 1, (groups_here + spots) * cluster_cap)
    rank = jnp.sum(place_of[None, :] < place_of[:, None], axis=1).astype(jnp.int32)
    cluster_at = place_of // cluster_cap
    first_slot = jnp.sum(cluster_at[None, :] < cluster_at[:, None], axis=1).astype(jnp.int32)
    at_rank = rank[None, :] == spots[:, None]
    order = jnp.sum(jnp.where(at_rank, spots[None, :], 0), axis=1).astype(jnp.int32)
    first = jnp.sum(jnp.where(at_rank, first_slot[None, :], 0), axis=1).astype(jnp.int32)

    lead = reach * block_len
    any_spec = pl.BlockSpec(memory_space=pl.ANY)
    smem_spec = pl.BlockSpec(memory_space=pltpu.SMEM)
    vmem_spec = pl.BlockSpec(memory_space=pltpu.VMEM)
    packed_shape = jax.ShapeDtypeStruct((slot_cap, block_len, seq_size * head_dim), jnp.bfloat16)
    results = pl.pallas_call(
        functools.partial(
            routed_kernel, seq_size, dp_size, slot_cap, block_len, head_dim, reach
        ),
        out_shape=(packed_shape,) * 4
        + (jax.ShapeDtypeStruct((groups_here, head_dim), jnp.float32),),
        in_specs=[smem_spec] * 3 + [vmem_spec] * 2 + [any_spec] * 4,
        out_specs=(any_spec,) * 4 + (vmem_spec,),
        scratch_shapes=[
            *[pltpu.VMEM((slots, block_len, head_dim), jnp.bfloat16)] * 4,
            pltpu.VMEM((4, lead + slots * block_len, head_dim), jnp.bfloat16),
            pltpu.VMEM((lead + slots * block_len, head_dim), jnp.float32),
            pltpu.VMEM((lead + slots * block_len, head_dim), jnp.float32),
            pltpu.VMEM((4, slots, block_len, head_dim), jnp.bfloat16),
            pltpu.VMEM((4, slots, block_len, head_dim), jnp.bfloat16),
            pltpu.VMEM((slots, head_dim), jnp.float32),
            pltpu.VMEM((dp_size, groups_here, head_dim), jnp.float32),
        ]
        + [pltpu.SemaphoreType.DMA((4,))] * 6
        + [pltpu.SemaphoreType.DMA((dp_size,))] * 2,
        compiler_params=pltpu.CompilerParams(
            collective_id=0, has_side_effects=True, vmem_limit_bytes=48 * 1024 * 1024
        ),
    )(
        order, rank, first, slot_table, centroid_sums,
        pack(keys), pack(queries), pack(values), pack(cotangent),
    )
    return tuple(unpack(item) for item in results[:4]) + (results[4],)


def solution(mesh):
    in_specs = (
        P("dp", "seq", None),
        P("dp", "seq", None),
        P("dp", "seq", None),
        P("dp", "seq", None),
        P("dp", None, "seq"),
        P("dp", "seq", None),
        P("seq", None),
    )
    out_specs = (
        P("dp", "seq", None),
        P("dp", "seq", None),
        P("dp", "seq", None),
        P("dp", "seq", None),
        P("seq", None),
    )
    return jax.shard_map(
        per_device, mesh=mesh, in_specs=in_specs, out_specs=out_specs, check_vma=False
    )
```

time: 758 us -> 122 us (0.16); the launches traced: 745 us -> 120 us
  matrix products: 370 us -> 0 us
  local copies, waits for them, and re-layouts: 268 us -> 9.03 us
  Pallas kernels: 0 us -> 110 us
  starting transfers between devices: 48.6 us -> 0 us
  waiting for transfers between devices: 39.9 us -> 0 us
  between operations: 14.8 us -> 0.68 us
    dot_general x105 -> x0, matrix products: 269 us -> none  [the longest x32 100 us: forward_tiles(): jnp.einsum('crs,csd->crd', weights, v_tiles, preferred_element_type=jnp.f...]
    scatter x4 -> x0, local copies, waits for them, and re-layouts: 178 us -> none  [from_tiles(): flat_rows.at[drop_row]]
    pallas_call x0 -> x1, Pallas kernels: none -> 110 us  [per_device(): pl.pallas_call(functools.partial(routed_kernel, seq_size, dp_size, slot_c...]
    sub x32 -> x0, matrix products: 101 us -> none  [forward_tiles(): raised = jnp.exp(scores - row_max)]
    gather x4 -> x0, local copies, waits for them, and re-layouts: 52.3 us -> none  [to_tiles(): return flat_rows[recv_row].reshape(groups_here, tile_rows, head_dim)]
    all_to_all x8 -> x0, starting transfers between devices: 48.5 us -> none  [the longest x3 21.1 us: per_device(): lax.all_to_all(shortened(tuple((from_tiles(item) for item in gradients)))...]
    all_to_all x8 -> x0, waiting for transfers between devices: 39.9 us -> none  [the longest x1 12.3 us: per_device(): lax.all_to_all(pack(queries), 'seq', split_axis=0, concat_axis=0, tiled=T...]
    another operation x12 -> x0, local copies, waits for them, and re-layouts: 22 us -> none
  transfers between devices with their start and end apart: 9 -> 0, of which waited for: 4 -> 0; matrix products, arithmetic and copies ran while one was open for 42% -> 0% of each run, Pallas kernels for 0% -> 0%
where the time goes in v1:
time: 122 us; the launch traced here: 120 us
  Pallas kernels  110 us (90%)
  local copies, waits for them, and re-layouts  9.03 us (7%)
    pallas_call x1, Pallas kernels, per_device(): pl.pallas_call(functools.partial(routed_kernel, seq_size, dp_size, slot_c...  110 us
    unnamed x18, local copies, waits for them, and re-layouts  8.92 us

profile of v1, /device:TPU:0, one launch (start us, length us, event | category | flops | bytes accessed | tf_op | source)
XLA Modules:
  0.0 119.8 jit_solution(11598901075282238456)
XLA Ops:
  0.6 0.0 copy-start.5
  0.7 0.7 copy-done.5
  1.3 0.0 copy-start.4
  1.3 0.1 copy.14
  1.4 0.1 eq.28
  1.5 0.1 select_reduce_fusion
  1.7 0.2 convert_reduce_fusion
  1.9 0.1 select_reduce_fusion.1
  2.0 0.2 copy-done.4
  2.2 0.0 copy-start
  2.2 1.0 copy-done
  3.2 0.0 copy-start.1
  3.2 1.0 copy-done.1
  4.2 0.0 copy-start.2
  4.2 1.0 copy-done.2
  5.3 0.0 copy-start.3
  5.3 1.0 copy-done.3
  6.3 109.6 %shard_map.101 = (bf16[2,64,2048]{2,1,0:T(8,128)(2,1)S(1)}, bf16[2,64,2048]{2,1,0:T(8,128)(2,1)S(1)}, bf16[2,64,2048]{2,1,0:T(8,128)(2,1)S(1)}, bf16[2,64,2048]{2,1,0:T(8,128)(2,1)S(1)}, f32[128,128]{1,0:T(8,128)S(1)}) custom-call(s32[32]{0:T(128)S(1)} %get-tuple-element.16.order_ref, s32[32]{0:T(128)S(1)} %get-tuple-element.20.rank_ref, ...), custom_call_target="tpu_custom_call" | custom-call | tf_op jit(solution)/shard_map/pallas_call | solution.py:294
  116.0 0.8 copy.21
  116.8 0.8 copy.22
  117.5 0.8 copy.23
  118.3 0.8 copy.24
  119.1 0.6 copy.25
  (2 shorter events, 0.0 us)
Async XLA Ops:
  0.6 0.7 copy-start.5
  1.3 0.8 copy-start.4
  2.2 1.0 copy-start
  3.2 1.0 copy-start.1
  4.2 1.0 copy-start.2
  5.3 1.0 copy-start.3

commit v2 on v1

--- a/solution.py
+++ b/solution.py
@@ -14,6 +14,7 @@
 PAIR = 2
 NT = (((1,), (1,)), ((), ()))
 TN = (((0,), (0,)), ((), ()))
+NN = (((1,), (0,)), ((), ()))
 
 
 def dot_f32(a, b, dims):
@@ -24,7 +25,7 @@
     seq_size, dp_size, slot_cap, block_len, head_dim, reach,
     order_ref, rank_ref, first_ref, slots_ref, cent_ref, k_ref, q_ref, v_ref, d_ref,
     out_ref, gq_ref, gk_ref, gv_ref, next_ref,
-    k_in, q_in, v_in, d_in, ordered, acc_k, acc_v, made, back, key_rows, sums,
+    k_in, q_in, v_in, d_in, ordered, probs_at, full_at, acc_k, acc_v, made, back, key_rows, sums,
     in_send, in_recv, in_own, back_send, back_recv, back_own, sum_send, sum_recv,
 ):
     my_dp = lax.axis_index("dp")
@@ -85,96 +86,35 @@
     def bytes_of(at):
         return arrived[at].at[pl.ds(0, others)]
 
-    for at, source in enumerate(sources):
+    def collect(at):
         part = bytes_of(at)
         pltpu.make_async_copy(part, part, in_recv.at[at]).wait()
         pltpu.make_async_copy(
-            source.at[:, :, columns(me)], arrived[at].at[rows_of(me)], in_own.at[at]
+            sources[at].at[:, :, columns(me)], arrived[at].at[rows_of(me)], in_own.at[at]
         ).wait()
 
-        def place(spot, carry, at=at):
+        def place(spot, carry):
             rows = pl.ds(pl.multiple_of(lead + spot * block_len, block_len), block_len)
             ordered[at, rows, :] = arrived[at][order_ref[spot]]
-            if at == 0:
-                key_rows[pl.ds(spot, 1), :] = jnp.sum(
-                    k_in[spot].astype(jnp.float32), axis=0, keepdims=True
-                )
             return carry
 
-        lax.fori_loop(0, slots, place, 0)
-        if at == 0:
-            groups = slots_ref.shape[0]
-            spots = lax.broadcasted_iota(jnp.int32, (groups, slots), 1)
-            member = jnp.zeros((groups, slots), jnp.float32)
-            for one in range(slots_ref.shape[1]):
-                member += jnp.where(slots_ref[:, one : one + 1] == spots, 1.0, 0.0)
-            sums[my_dp] = lax.dot_general(
-                member, key_rows[...], (((1,), (0,)), ((), ())),
-                precision=lax.Precision.HIGHEST, preferred_element_type=jnp.float32,
-            )
-            for step in range(1, dp_size):
-                target = lax.rem(my_dp + step, dp_size)
-                pltpu.make_async_remote_copy(
-                    src_ref=sums.at[my_dp],
-                    dst_ref=sums.at[my_dp],
-                    send_sem=sum_send.at[step],
-                    recv_sem=sum_recv.at[step],
-                    device_id=(target, me),
-                    device_id_type=MESH,
-                ).start()
-
-    row_at = lax.broadcasted_iota(jnp.int32, (tile, window), 0)
-    col_at = lax.broadcasted_iota(jnp.int32, (tile, window), 1)
-    below = col_at <= row_at + lead
-    row_one = lax.broadcasted_iota(jnp.int32, (tile, 1), 0)
-
-    def attend(index, carry):
-        start = pl.multiple_of(index * tile, tile)
-        own = pl.ds(pl.multiple_of(start + lead, block_len), tile)
-        near = pl.ds(start, window)
-        k = ordered[0, near, :]
-        q = ordered[1, own, :]
-        v = ordered[2, near, :]
-        g = ordered[3, own, :]
-        low = jnp.zeros((tile, 1), jnp.int32)
-        for one in range(PAIR):
-            edge = lead + (first_ref[index * PAIR + one] - index * PAIR) * block_len
-            low = jnp.where(row_one >= one * block_len, edge, low)
-        visible = below & (col_at >= low)
-        scores = jnp.where(visible, dot_f32(q, k, NT) * score_scale, neg_fill)
-        raised = jnp.exp(scores - jnp.max(scores, axis=-1, keepdims=True))
-        probs = raised / jnp.sum(raised, axis=-1, keepdims=True)
-        weights = probs.astype(jnp.bfloat16)
-        out_full = dot_f32(weights, v, (((1,), (0,)), ((), ())))
-        dprobs = dot_f32(g, v, NT)
-        row_dot = jnp.sum(g.astype(jnp.float32) * out_full, axis=-1, keepdims=True)
-        dscores = (probs * (dprobs - row_dot) * score_scale).astype(jnp.bfloat16)
-        here = pl.ds(index * PAIR, PAIR)
-        tiled = (PAIR, block_len, head_dim)
-        grad_q = dot_f32(dscores, k, (((1,), (0,)), ((), ())))
-        made[0, here] = out_full.astype(jnp.bfloat16).reshape(tiled)
-        made[1, here] = grad_q.astype(jnp.bfloat16).reshape(tiled)
-        acc_k[near, :] += dot_f32(dscores, q, TN)
-        acc_v[near, :] += dot_f32(weights, g, TN)
-        return carry
-
-    lax.fori_loop(0, slots // PAIR, attend, 0)
-    made[2] = acc_k[lead:, :].astype(jnp.bfloat16).reshape(slots, block_len, head_dim)
-    made[3] = acc_v[lead:, :].astype(jnp.bfloat16).reshape(slots, block_len, head_dim)
+        lax.fori_loop(0, slots, place, 0, unroll=4)
 
     results = (out_ref, gq_ref, gk_ref, gv_ref)
-    for at, result in enumerate(results):
-
-        def settle(spot, carry, at=at):
+
+    def give_back(at):
+        result = results[at]
+
+        def settle(spot, carry):
             back[at, spot] = made[at, rank_ref[spot]]
             return carry
 
-        lax.fori_loop(0, slots, settle, 0)
+        lax.fori_loop(0, slots, settle, 0, unroll=4)
         pltpu.make_async_copy(
             back.at[at, rows_of(me)], result.at[:, :, columns(me)], back_own.at[at]
         ).start()
 
-        def give(step, carry, at=at, result=result):
+        def give(step, carry):
             target = lax.rem(me + step, seq_size)
             pltpu.make_async_remote_copy(
                 src_ref=back.at[at, rows_of(target)],
@@ -188,6 +128,87 @@
 
         lax.fori_loop(1, seq_size, give, 0)
 
+    row_at = lax.broadcasted_iota(jnp.int32, (tile, window), 0)
+    col_at = lax.broadcasted_iota(jnp.int32, (tile, window), 1)
+    row_one = lax.broadcasted_iota(jnp.int32, (tile, 1), 0)
+    tiled = (PAIR, block_len, head_dim)
+
+    def spans(index):
+        start = pl.multiple_of(index * tile, tile)
+        own = pl.ds(pl.multiple_of(start + lead, block_len), tile)
+        return own, pl.ds(start, window), pl.ds(index * PAIR, PAIR)
+
+    def forward(index, carry):
+        own, near, here = spans(index)
+        low = jnp.zeros((tile, 1), jnp.int32)
+        for one in range(PAIR):
+            edge = lead + (first_ref[index * PAIR + one] - index * PAIR) * block_len
+            low = jnp.where(row_one >= one * block_len, edge, low)
+        visible = (col_at <= row_at + lead) & (col_at >= low)
+        scores = dot_f32(ordered[1, own, :], ordered[0, near, :], NT) * score_scale
+        scores = jnp.where(visible, scores, neg_fill)
+        raised = jnp.exp(scores - jnp.max(scores, axis=-1, keepdims=True))
+        probs = raised / jnp.sum(raised, axis=-1, keepdims=True)
+        out_full = dot_f32(probs.astype(jnp.bfloat16), ordered[2, near, :], NN)
+        probs_at[index] = probs
+        full_at[index] = out_full
+        made[0, here] = out_full.astype(jnp.bfloat16).reshape(tiled)
+        return carry
+
+    def backward(index, carry):
+        own, near, here = spans(index)
+        k = ordered[0, near, :]
+        q = ordered[1, own, :]
+        g = ordered[3, own, :]
+        probs = probs_at[index]
+        dprobs = dot_f32(g, ordered[2, near, :], NT)
+        row_dot = jnp.sum(g.astype(jnp.float32) * full_at[index], axis=-1, keepdims=True)
+        dscores = (probs * (dprobs - row_dot) * score_scale).astype(jnp.bfloat16)
+        made[1, here] = dot_f32(dscores, k, NN).astype(jnp.bfloat16).reshape(tiled)
+        acc_k[near, :] += dot_f32(dscores, q, TN)
+        acc_v[near, :] += dot_f32(probs.astype(jnp.bfloat16), g, TN)
+        return carry
+
+    collect(0)
+    collect(1)
+    collect(2)
+    lax.fori_loop(0, slots // PAIR, forward, 0, unroll=4)
+    give_back(0)
+    collect(3)
+    lax.fori_loop(0, slots // PAIR, backward, 0, unroll=2)
+    give_back(1)
+    made[2] = acc_k[lead:, :].astype(jnp.bfloat16).reshape(slots, block_len, head_dim)
+    give_back(2)
+    made[3] = acc_v[lead:, :].astype(jnp.bfloat16).reshape(slots, block_len, head_dim)
+    give_back(3)
+
+    def add_keys(spot, carry):
+        key_rows[pl.ds(spot, 1), :] = jnp.sum(
+            k_in[spot].astype(jnp.float32), axis=0, keepdims=True
+        )
+        return carry
+
+    lax.fori_loop(0, slots, add_keys, 0)
+    groups = slots_ref.shape[0]
+    spots = lax.broadcasted_iota(jnp.int32, (groups, slots), 1)
+    member = jnp.zeros((groups, slots), jnp.float32)
+    for one in range(slots_ref.shape[1]):
+        member += jnp.where(slots_ref[:, one : one + 1] == spots, 1.0, 0.0)
+    sums[my_dp] = lax.dot_general(
+        member, key_rows[...], NN,
+        precision=lax.Precision.HIGHEST, preferred_element_type=jnp.float32,
+    )
+    for step in range(1, dp_size):
+        target = lax.rem(my_dp + step, dp_size)
+        pltpu.make_async_remote_copy(
+            src_ref=sums.at[my_dp],
+            dst_ref=sums.at[my_dp],
+            send_sem=sum_send.at[step],
+            recv_sem=sum_recv.at[step],
+            device_id=(target, me),
+            device_id_type=MESH,
+        ).start()
+
     for step in range(1, dp_size):
         source_dp = lax.rem(my_dp - step + dp_size, dp_size)
         swap = pltpu.make_async_remote_copy(
@@ -213,6 +234,18 @@
         pltpu.make_async_copy(
             back.at[at, rows_of(me)], result.at[:, :, columns(me)], back_own.at[at]
         ).wait()
+
+
+def settle_kernel(*refs):
+    held, results, done = refs[:5], refs[5:10], refs[10]
+    copies = [
+        pltpu.make_async_copy(source, result, done.at[at])
+        for at, (source, result) in enumerate(zip(held, results))
+    ]
+    for copy in copies:
+        copy.start()
+    for copy in copies:
+        copy.wait()
 
 
 def per_device(queries, keys, values, cotangent, cluster_of, block_list, centroid_sums):
@@ -297,11 +330,13 @@
         ),
         out_shape=(packed_shape,) * 4
         + (jax.ShapeDtypeStruct((groups_here, head_dim), jnp.float32),),
-        in_specs=[smem_spec] * 3 + [vmem_spec] * 2 + [any_spec] * 4,
+        in_specs=[smem_spec] * 3 + [vmem_spec] * 2 + [pl.BlockSpec(memory_space=pltpu.HBM)] * 4,
         out_specs=(any_spec,) * 4 + (vmem_spec,),
         scratch_shapes=[
             *[pltpu.VMEM((slots, block_len, head_dim), jnp.bfloat16)] * 4,
             pltpu.VMEM((4, lead + slots * block_len, head_dim), jnp.bfloat16),
+            pltpu.VMEM((slots // PAIR, PAIR * block_len, lead + PAIR * block_len), jnp.float32),
+            pltpu.VMEM((slots // PAIR, PAIR * block_len, head_dim), jnp.float32),
             pltpu.VMEM((lead + slots * block_len, head_dim), jnp.float32),
             pltpu.VMEM((lead + slots * block_len, head_dim), jnp.float32),
             pltpu.VMEM((4, slots, block_len, head_dim), jnp.bfloat16),
@@ -312,12 +347,21 @@
         + [pltpu.SemaphoreType.DMA((4,))] * 6
         + [pltpu.SemaphoreType.DMA((dp_size,))] * 2,
         compiler_params=pltpu.CompilerParams(
-            collective_id=0, has_side_effects=True, vmem_limit_bytes=48 * 1024 * 1024
+            collective_id=0, has_side_effects=True, vmem_limit_bytes=60 * 1024 * 1024
         ),
     )(
         order, rank, first, slot_table, centroid_sums,
         pack(keys), pack(queries), pack(values), pack(cotangent),
     )
+    if owner_count == 1:
+        results = pl.pallas_call(
+            settle_kernel,
+            out_shape=tuple(jax.ShapeDtypeStruct(item.shape, item.dtype) for item in results),
+            in_specs=[any_spec] * 5,
+            out_specs=(any_spec,) * 5,
+            scratch_shapes=[pltpu.SemaphoreType.DMA((5,))],
+            compiler_params=pltpu.CompilerParams(vmem_limit_bytes=60 * 1024 * 1024),
+        )(*results)
     return tuple(unpack(item) for item in results[:4]) + (results[4],)
 
 

time: 122 us -> 170 us (1.39)
  Pallas kernels: 110 us -> 165 us
  local copies, waits for them, and re-layouts: 9.03 us -> 1.39 us
    pallas_call x0 -> x1, Pallas kernels: none -> 66.7 us  [per_device(): pl.pallas_call(settle_kernel, out_shape=tuple((jax.ShapeDtypeStruct(item....]
    pallas_call x1, Pallas kernels: 110 us -> 98.2 us  [per_device(): pl.pallas_call(functools.partial(routed_kernel, seq_size, dp_size, slot_c...]
    unnamed x18 -> x7, local copies, waits for them, and re-layouts: 8.92 us -> 1.29 us
where the time goes in v2:
time: 170 us; the launch traced here: 168 us
  Pallas kernels  165 us (97%)
    pallas_call x1, Pallas kernels, per_device(): pl.pallas_call(functools.partial(routed_kernel, seq_size, dp_size, slot_c...  98.2 us
    pallas_call x1, Pallas kernels, per_device(): pl.pallas_call(settle_kernel, out_shape=tuple((jax.ShapeDtypeStruct(item....  66.7 us

profile of v2, /device:TPU:0, one launch (start us, length us, event | category | flops | bytes accessed | tf_op | source)
XLA Modules:
  0.0 167.9 jit_solution(9162258732774469533)
XLA Ops:
  0.6 0.0 copy-start.2
  0.7 0.7 copy-done.2
  1.3 0.1 copy.14
  1.4 0.0 copy-start
  1.4 0.1 eq.28
  1.5 0.1 select_reduce_fusion
  1.7 0.2 convert_reduce_fusion
  1.9 0.0 copy-start.1
  1.9 0.5 copy-done.1
  2.4 0.6 select_reduce_fusion.1
  3.0 0.0 copy-done
  3.0 98.2 %shard_map.101 = (bf16[2,64,2048]{2,1,0:T(8,128)(2,1)}, bf16[2,64,2048]{2,1,0:T(8,128)(2,1)}, bf16[2,64,2048]{2,1,0:T(8,128)(2,1)}, bf16[2,64,2048]{2,1,0:T(8,128)(2,1)}, f32[128,128]{1,0:T(8,128)}) custom-call(s32[32]{0:T(128)} %get-tuple-element.26.order_ref, s32[32]{0:T(128)} %copy-done.1, s32[32]{0:T(128)} %get-tuple-element.25.first_ref, ...), custom_call_target="tpu_custom_call" | custom-call | tf_op jit(solution)/shard_map/pallas_call | solution.py:327
  101.2 66.7 %shard_map.102 = (bf16[2,64,2048]{2,1,0:T(8,128)(2,1)}, bf16[2,64,2048]{2,1,0:T(8,128)(2,1)}, bf16[2,64,2048]{2,1,0:T(8,128)(2,1)}, bf16[2,64,2048]{2,1,0:T(8,128)(2,1)}, f32[128,128]{1,0:T(8,128)}) custom-call(bf16[2,64,2048]{2,1,0:T(8,128)(2,1)} %get-tuple-element.15.refs_0_, bf16[2,64,2048]{2,1,0:T(8,128)(2,1)} %get-tuple-element.16.refs_1_, ...), custom_call_target="tpu_custom_call" | custom-call | tf_op jit(solution)/shard_map/pallas_call | solution.py:357
  (2 shorter events, 0.0 us)
Async XLA Ops:
  0.6 0.7 copy-start.2
  1.4 1.6 copy-start
  1.9 0.5 copy-start.1

commit v3 on v2

--- a/solution.py
+++ b/solution.py
@@ -52,6 +52,18 @@
         )
     pl.semaphore_wait(barrier, seq_size + dp_size - 2)
 
+    def partner(step):
+        if seq_size & (seq_size - 1):
+            return lax.rem(me + step, seq_size)
+        odd = lax.rem(step, 2)
+        offset = odd * (seq_size // 2) + step // 2
+        target = 0
+        for bit in range(seq_size.bit_length() - 1):
+            mine = lax.rem(me // (1 << bit), 2)
+            other = lax.rem(offset // (1 << bit), 2)
+            target = target + (mine + other - 2 * mine * other) * (1 << bit)
+        return target
+
     def columns(index):
         return pl.ds(pl.multiple_of(index * head_dim, head_dim), head_dim)
 
@@ -66,7 +78,7 @@
         ).start()
 
         def send(step, carry, at=at, source=source):
-            target = lax.rem(me + step, seq_size)
+            target = partner(step)
             pltpu.make_async_remote_copy(
                 src_ref=source.at[:, :, columns(target)],
                 dst_ref=arrived[at].at[rows_of(me)],
@@ -115,7 +127,7 @@
         ).start()
 
         def give(step, carry):
-            target = lax.rem(me + step, seq_size)
+            target = partner(step)
             pltpu.make_async_remote_copy(
                 src_ref=back.at[at, rows_of(target)],
                 dst_ref=result.at[:, :, columns(me)],
@@ -237,15 +249,20 @@
 
 
 def settle_kernel(*refs):
-    held, results, done = refs[:5], refs[5:10], refs[10]
-    copies = [
-        pltpu.make_async_copy(source, result, done.at[at])
-        for at, (source, result) in enumerate(zip(held, results))
+    held, results, staged, loaded, stored = refs[:5], refs[5:10], refs[10:15], refs[15], refs[16]
+    loads = [
+        pltpu.make_async_copy(held[at], staged[at], loaded.at[at]) for at in range(5)
     ]
-    for copy in copies:
-        copy.start()
-    for copy in copies:
-        copy.wait()
+    stores = [
+        pltpu.make_async_copy(staged[at], results[at], stored.at[at]) for at in range(5)
+    ]
+    for load in loads:
+        load.start()
+    for load, store in zip(loads, stores):
+        load.wait()
+        store.start()
+    for store in stores:
+        store.wait()
 
 
 def per_device(queries, keys, values, cotangent, cluster_of, block_list, centroid_sums):
@@ -359,7 +376,8 @@
             out_shape=tuple(jax.ShapeDtypeStruct(item.shape, item.dtype) for item in results),
             in_specs=[any_spec] * 5,
             out_specs=(any_spec,) * 5,
-            scratch_shapes=[pltpu.SemaphoreType.DMA((5,))],
+            scratch_shapes=[pltpu.VMEM(item.shape, item.dtype) for item in results]
+            + [pltpu.SemaphoreType.DMA((5,))] * 2,
             compiler_params=pltpu.CompilerParams(vmem_limit_bytes=60 * 1024 * 1024),
         )(*results)
     return tuple(unpack(item) for item in results[:4]) + (results[4],)

time: 170 us -> 106 us (0.62); the launches traced: 168 us -> 106 us
  Pallas kernels: 165 us -> 103 us
    pallas_call x1, Pallas kernels: 66.7 us -> 2.45 us  [per_device(): pl.pallas_call(settle_kernel, out_shape=tuple((jax.ShapeDtypeStruct(item....]
    pallas_call x1, Pallas kernels: 98.2 us -> 100 us  [per_device(): pl.pallas_call(functools.partial(routed_kernel, seq_size, dp_size, slot_c...]
where the time goes in v3:
time: 106 us
  Pallas kernels  103 us (97%)
  local copies, waits for them, and re-layouts  1.39 us (1%)
    pallas_call x1, Pallas kernels, per_device(): pl.pallas_call(functools.partial(routed_kernel, seq_size, dp_size, slot_c...  100 us
    pallas_call x1, Pallas kernels, per_device(): pl.pallas_call(settle_kernel, out_shape=tuple((jax.ShapeDtypeStruct(item....  2.45 us

profile of v3, /device:TPU:0, one launch (start us, length us, event | category | flops | bytes accessed | tf_op | source)
XLA Modules:
  0.0 105.6 jit_solution(1458644694417533878)
XLA Ops:
  0.6 0.0 copy-start.2
  0.7 0.7 copy-done.2
  1.3 0.1 copy.14
  1.4 0.0 copy-start
  1.4 0.1 eq.28
  1.5 0.1 select_reduce_fusion
  1.7 0.2 convert_reduce_fusion
  1.9 0.0 copy-start.1
  1.9 0.5 copy-done.1
  2.4 0.6 select_reduce_fusion.1
  3.0 0.0 copy-done
  3.0 100.2 %shard_map.101 = (bf16[2,64,2048]{2,1,0:T(8,128)(2,1)}, bf16[2,64,2048]{2,1,0:T(8,128)(2,1)}, bf16[2,64,2048]{2,1,0:T(8,128)(2,1)}, bf16[2,64,2048]{2,1,0:T(8,128)(2,1)}, f32[128,128]{1,0:T(8,128)}) custom-call(s32[32]{0:T(128)} %get-tuple-element.26.order_ref, s32[32]{0:T(128)} %copy-done.1, s32[32]{0:T(128)} %get-tuple-element.25.first_ref, ...), custom_call_target="tpu_custom_call" | custom-call | tf_op jit(solution)/shard_map/pallas_call | solution.py:344
  103.2 2.4 %shard_map.102 = (bf16[2,64,2048]{2,1,0:T(8,128)(2,1)}, bf16[2,64,2048]{2,1,0:T(8,128)(2,1)}, bf16[2,64,2048]{2,1,0:T(8,128)(2,1)}, bf16[2,64,2048]{2,1,0:T(8,128)(2,1)}, f32[128,128]{1,0:T(8,128)}) custom-call(bf16[2,64,2048]{2,1,0:T(8,128)(2,1)} %get-tuple-element.15.refs_0_, bf16[2,64,2048]{2,1,0:T(8,128)(2,1)} %get-tuple-element.16.refs_1_, ...), custom_call_target="tpu_custom_call" | custom-call | tf_op jit(solution)/shard_map/pallas_call | solution.py:374
  (2 shorter events, 0.0 us)
Async XLA Ops:
  0.6 0.7 copy-start.2
  1.4 1.6 %copy-start = (s32[1,128,4]{2,1,0:T(8,128)}, s32[1,128,4]{2,1,0:T(8,128)S(1)}, u32[]{:S(2)}) copy-start(s32[1,128,4]{2,1,0:T(8,128)S(1)} %copy.14) | copy-start | bytes 6148
  1.9 0.5 copy-start.1

commit v4 on v3

--- a/solution.py
+++ b/solution.py
@@ -23,10 +23,10 @@
 
 def routed_kernel(
     seq_size, dp_size, slot_cap, block_len, head_dim, reach,
-    order_ref, rank_ref, first_ref, slots_ref, cent_ref, k_ref, q_ref, v_ref, d_ref,
+    slots_ref, cent_ref, k_ref, q_ref, v_ref, d_ref,
     out_ref, gq_ref, gk_ref, gv_ref, next_ref,
-    k_in, q_in, v_in, d_in, ordered, probs_at, full_at, acc_k, acc_v, made, back, key_rows, sums,
-    in_send, in_recv, in_own, back_send, back_recv, back_own, sum_send, sum_recv,
+    k_in, q_in, v_in, d_in, ordered, probs_at, full_at, acc_k, acc_v, made, back, key_rows, sums, drawn, table,
+    in_send, in_recv, in_own, back_send, back_recv, back_own, sum_send, sum_recv, table_sem,
 ):
     my_dp = lax.axis_index("dp")
     me = lax.axis_index("seq")
@@ -72,12 +72,13 @@
 
     sources = (k_ref, q_ref, v_ref, d_ref)
     arrived = (k_in, q_in, v_in, d_in)
-    for at, source in enumerate(sources):
+    def send_out(at):
+        source = sources[at]
         pltpu.make_async_copy(
             source.at[:, :, columns(me)], arrived[at].at[rows_of(me)], in_own.at[at]
         ).start()
 
-        def send(step, carry, at=at, source=source):
+        def send(step, carry):
             target = partner(step)
             pltpu.make_async_remote_copy(
                 src_ref=source.at[:, :, columns(target)],
@@ -91,6 +92,47 @@
 
         lax.fori_loop(1, seq_size, send, 0)
 
+    send_out(0)
+    send_out(1)
+
+    cap, groups = slots_ref.shape
+    lanes = drawn.shape[1]
+    slot_at = lax.broadcasted_iota(jnp.int32, (slots, groups), 0)
+    group_at = lax.broadcasted_iota(jnp.int32, (slots, groups), 1)
+    place_col = jnp.zeros((slots, 1), jnp.int32)
+    group_col = jnp.zeros((slots, 1), jnp.int32)
+    member = jnp.zeros((slots, groups), jnp.float32)
+    for one in range(cap):
+        holds = slots_ref[one : one + 1, :] == slot_at
+        member += jnp.where(holds, 1.0, 0.0)
+        place_col += jnp.sum(
+            jnp.where(holds, group_at * cap + one + 1, 0), axis=1, keepdims=True
+        )
+        group_col += jnp.sum(jnp.where(holds, group_at + 1, 0), axis=1, keepdims=True)
+    spot_col = lax.broadcasted_iota(jnp.int32, (slots, 1), 0)
+    place_col = jnp.where(place_col > 0, place_col, (groups + spot_col) * cap + 1)
+    group_col = jnp.where(group_col > 0, group_col, groups + spot_col + 1)
+    spot_at = lax.broadcasted_iota(jnp.int32, (slots, lanes), 0)
+    lane_at = lax.broadcasted_iota(jnp.int32, (slots, lanes), 1)
+
+    def lay(column):
+        return jnp.sum(jnp.where(spot_at == lane_at, column, 0), axis=0, keepdims=True)
+
+    def count(column):
+        less = (lay(column) < column) & (lane_at < slots)
+        return jnp.sum(jnp.where(less, 1, 0), axis=1, keepdims=True)
+
+    rank_col = count(place_col)
+    first_col = count(group_col)
+    at_rank = rank_col == lane_at
+    drawn[...] = jnp.zeros_like(drawn)
+    drawn[0:1, :] = jnp.sum(jnp.where(at_rank, spot_at, 0), axis=0, keepdims=True)
+    drawn[1:2, :] = lay(rank_col)
+    drawn[2:3, :] = jnp.sum(jnp.where(at_rank, first_col, 0), axis=0, keepdims=True)
+    fill = pltpu.make_async_copy(drawn, table, table_sem.at[0])
+    fill.start()
+    fill.wait()
+
     ordered[:, :lead, :] = jnp.zeros((4, lead, head_dim), jnp.bfloat16)
     acc_k[...] = jnp.zeros_like(acc_k)
     acc_v[...] = jnp.zeros_like(acc_v)
@@ -107,7 +149,7 @@
 
         def place(spot, carry):
             rows = pl.ds(pl.multiple_of(lead + spot * block_len, block_len), block_len)
-            ordered[at, rows, :] = arrived[at][order_ref[spot]]
+            ordered[at, rows, :] = arrived[at][table[0, spot]]
             return carry
 
         lax.fori_loop(0, slots, place, 0, unroll=4)
@@ -118,7 +160,7 @@
         result = results[at]
 
         def settle(spot, carry):
-            back[at, spot] = made[at, rank_ref[spot]]
+            back[at, spot] = made[at, table[1, spot]]
             return carry
 
         lax.fori_loop(0, slots, settle, 0, unroll=4)
@@ -154,7 +196,7 @@
         own, near, here = spans(index)
         low = jnp.zeros((tile, 1), jnp.int32)
         for one in range(PAIR):
-            edge = lead + (first_ref[index * PAIR + one] - index * PAIR) * block_len
+            edge = lead + (table[2, index * PAIR + one] - index * PAIR) * block_len
             low = jnp.where(row_one >= one * block_len, edge, low)
         visible = (col_at <= row_at + lead) & (col_at >= low)
         scores = dot_f32(ordered[1, own, :], ordered[0, near, :], NT) * score_scale
@@ -178,21 +220,34 @@
         dscores = (probs * (dprobs - row_dot) * score_scale).astype(jnp.bfloat16)
         made[1, here] = dot_f32(dscores, k, NN).astype(jnp.bfloat16).reshape(tiled)
         acc_k[near, :] += dot_f32(dscores, q, TN)
-        acc_v[near, :] += dot_f32(probs.astype(jnp.bfloat16), g, TN)
         return carry
 
+    def backward_v(index, carry):
+        own, near, here = spans(index)
+        acc_v[near, :] += dot_f32(probs_at[index].astype(jnp.bfloat16), ordered[3, own, :], TN)
+        return carry
+
+    def wait_sent(at):
+        moved = bytes_of(at)
+        pltpu.make_async_copy(moved, moved, in_send.at[at]).wait()
+
+    wait_sent(0)
+    send_out(2)
+    wait_sent(1)
+    send_out(3)
     collect(0)
     collect(1)
     collect(2)
     lax.fori_loop(0, slots // PAIR, forward, 0, unroll=4)
     give_back(0)
     collect(3)
+    lax.fori_loop(0, slots // PAIR, backward_v, 0, unroll=2)
+    made[3] = acc_v[lead:, :].astype(jnp.bfloat16).reshape(slots, block_len, head_dim)
+    give_back(3)
     lax.fori_loop(0, slots // PAIR, backward, 0, unroll=2)
     give_back(1)
     made[2] = acc_k[lead:, :].astype(jnp.bfloat16).reshape(slots, block_len, head_dim)
     give_back(2)
-    made[3] = acc_v[lead:, :].astype(jnp.bfloat16).reshape(slots, block_len, head_dim)
-    give_back(3)
 
     def add_keys(spot, carry):
         key_rows[pl.ds(spot, 1), :] = jnp.sum(
@@ -201,13 +256,8 @@
         return carry
 
     lax.fori_loop(0, slots, add_keys, 0)
-    groups = slots_ref.shape[0]
-    spots = lax.broadcasted_iota(jnp.int32, (groups, slots), 1)
-    member = jnp.zeros((groups, slots), jnp.float32)
-    for one in range(slots_ref.shape[1]):
-        member += jnp.where(slots_ref[:, one : one + 1] == spots, 1.0, 0.0)
     sums[my_dp] = lax.dot_general(
-        member, key_rows[...], NN,
+        member, key_rows[...], TN,
         precision=lax.Precision.HIGHEST, preferred_element_type=jnp.float32,
     )
     for step in range(1, dp_size):
@@ -239,8 +289,9 @@
     next_ref[...] = decay_rate * cent_ref[...] + (1.0 - decay_rate) * total
 
     for at, result in enumerate(results):
+        if at > 1:
+            wait_sent(at)
         moved = bytes_of(at)
-        pltpu.make_async_copy(moved, moved, in_send.at[at]).wait()
         pltpu.make_async_copy(moved, moved, back_recv.at[at]).wait()
         pltpu.make_async_copy(moved, moved, back_send.at[at]).wait()
         pltpu.make_async_copy(
@@ -324,21 +375,9 @@
         slot_table = jnp.where(flat >= 0, source_dev * slot_cap + slot_at, -1)
         slot_table = slot_table.reshape(members.shape).astype(jnp.int32)
 
-    spots = jnp.arange(slots, dtype=jnp.int32)
-    holds = slot_table.reshape(-1)[:, None] == spots[None, :]
-    place = jnp.arange(holds.shape[0], dtype=jnp.int32)
-    place_of = jnp.sum(jnp.where(holds, place[:, None] + 1, 0), axis=0)
-    place_of = jnp.where(place_of > 0, place_of - 1, (groups_here + spots) * cluster_cap)
-    rank = jnp.sum(place_of[None, :] < place_of[:, None], axis=1).astype(jnp.int32)
-    cluster_at = place_of // cluster_cap
-    first_slot = jnp.sum(cluster_at[None, :] < cluster_at[:, None], axis=1).astype(jnp.int32)
-    at_rank = rank[None, :] == spots[:, None]
-    order = jnp.sum(jnp.where(at_rank, spots[None, :], 0), axis=1).astype(jnp.int32)
-    first = jnp.sum(jnp.where(at_rank, first_slot[None, :], 0), axis=1).astype(jnp.int32)
-
     lead = reach * block_len
+    lanes = -(-slots // 128) * 128
     any_spec = pl.BlockSpec(memory_space=pl.ANY)
-    smem_spec = pl.BlockSpec(memory_space=pltpu.SMEM)
     vmem_spec = pl.BlockSpec(memory_space=pltpu.VMEM)
     packed_shape = jax.ShapeDtypeStruct((slot_cap, block_len, seq_size * head_dim), jnp.bfloat16)
     results = pl.pallas_call(
@@ -347,7 +386,7 @@
         ),
         out_shape=(packed_shape,) * 4
         + (jax.ShapeDtypeStruct((groups_here, head_dim), jnp.float32),),
-        in_specs=[smem_spec] * 3 + [vmem_spec] * 2 + [pl.BlockSpec(memory_space=pltpu.HBM)] * 4,
+        in_specs=[vmem_spec] * 2 + [pl.BlockSpec(memory_space=pltpu.HBM)] * 4,
         out_specs=(any_spec,) * 4 + (vmem_spec,),
         scratch_shapes=[
             *[pltpu.VMEM((slots, block_len, head_dim), jnp.bfloat16)] * 4,
@@ -360,14 +399,17 @@
             pltpu.VMEM((4, slots, block_len, head_dim), jnp.bfloat16),
             pltpu.VMEM((slots, head_dim), jnp.float32),
             pltpu.VMEM((dp_size, groups_here, head_dim), jnp.float32),
+            pltpu.VMEM((8, lanes), jnp.int32),
+            pltpu.SMEM((8, lanes), jnp.int32),
         ]
         + [pltpu.SemaphoreType.DMA((4,))] * 6
-        + [pltpu.SemaphoreType.DMA((dp_size,))] * 2,
+        + [pltpu.SemaphoreType.DMA((dp_size,))] * 2
+        + [pltpu.SemaphoreType.DMA((1,))],
         compiler_params=pltpu.CompilerParams(
             collective_id=0, has_side_effects=True, vmem_limit_bytes=60 * 1024 * 1024
         ),
     )(
-        order, rank, first, slot_table, centroid_sums,
+        slot_table.T, centroid_sums,
         pack(keys), pack(queries), pack(values), pack(cotangent),
     )
     if owner_count == 1:

time: 106 us -> 104 us (0.981)
  local copies, waits for them, and re-layouts: 1.39 us -> 0 us
    unnamed x7 -> x0, local copies, waits for them, and re-layouts: 1.29 us -> none
where the time goes in v4:
time: 104 us; the launch traced here: 103 us
  Pallas kernels  103 us (99%)
    pallas_call x1, Pallas kernels, per_device(): pl.pallas_call(functools.partial(routed_kernel, seq_size, dp_size, slot_c...  100 us
    pallas_call x1, Pallas kernels, per_device(): pl.pallas_call(settle_kernel, out_shape=tuple((jax.ShapeDtypeStruct(item....  2.45 us

profile of v4, /device:TPU:0, one launch (start us, length us, event | category | flops | bytes accessed | tf_op | source)
XLA Modules:
  0.0 103.3 jit_solution(4631560747094348110)
XLA Ops:
  0.6 100.2 %shard_map.101 = (bf16[2,64,2048]{2,1,0:T(8,128)(2,1)}, bf16[2,64,2048]{2,1,0:T(8,128)(2,1)}, bf16[2,64,2048]{2,1,0:T(8,128)(2,1)}, bf16[2,64,2048]{2,1,0:T(8,128)(2,1)}, f32[128,128]{1,0:T(8,128)}) custom-call(s32[4,128]{1,0:T(4,128)} %bitcast.15, f32[128,128]{1,0:T(8,128)} %cent_ref.1, bf16[2,64,2048]{2,1,0:T(8,128)(2,1)} %bitcast.11, ...), custom_call_target="tpu_custom_call" | custom-call | tf_op jit(solution)/shard_map/pallas_call | solution.py:383
  100.9 2.4 %shard_map.102 = (bf16[2,64,2048]{2,1,0:T(8,128)(2,1)}, bf16[2,64,2048]{2,1,0:T(8,128)(2,1)}, bf16[2,64,2048]{2,1,0:T(8,128)(2,1)}, bf16[2,64,2048]{2,1,0:T(8,128)(2,1)}, f32[128,128]{1,0:T(8,128)}) custom-call(bf16[2,64,2048]{2,1,0:T(8,128)(2,1)} %get-tuple-element.15.refs_0_, bf16[2,64,2048]{2,1,0:T(8,128)(2,1)} %get-tuple-element.16.refs_1_, ...), custom_call_target="tpu_custom_call" | custom-call | tf_op jit(solution)/shard_map/pallas_call | solution.py:416

commit v5 on v4

--- a/solution.py
+++ b/solution.py
@@ -94,6 +94,7 @@
 
     send_out(0)
     send_out(1)
+    send_out(2)
 
     cap, groups = slots_ref.shape
     lanes = drawn.shape[1]
@@ -232,22 +233,9 @@
         pltpu.make_async_copy(moved, moved, in_send.at[at]).wait()
 
     wait_sent(0)
-    send_out(2)
-    wait_sent(1)
     send_out(3)
     collect(0)
     collect(1)
-    collect(2)
-    lax.fori_loop(0, slots // PAIR, forward, 0, unroll=4)
-    give_back(0)
-    collect(3)
-    lax.fori_loop(0, slots // PAIR, backward_v, 0, unroll=2)
-    made[3] = acc_v[lead:, :].astype(jnp.bfloat16).reshape(slots, block_len, head_dim)
-    give_back(3)
-    lax.fori_loop(0, slots // PAIR, backward, 0, unroll=2)
-    give_back(1)
-    made[2] = acc_k[lead:, :].astype(jnp.bfloat16).reshape(slots, block_len, head_dim)
-    give_back(2)
 
     def add_keys(spot, carry):
         key_rows[pl.ds(spot, 1), :] = jnp.sum(
@@ -271,6 +259,18 @@
             device_id_type=MESH,
         ).start()
 
+    collect(2)
+    lax.fori_loop(0, slots // PAIR, forward, 0, unroll=4)
+    give_back(0)
+    collect(3)
+    lax.fori_loop(0, slots // PAIR, backward_v, 0, unroll=2)
+    made[3] = acc_v[lead:, :].astype(jnp.bfloat16).reshape(slots, block_len, head_dim)
+    give_back(3)
+    lax.fori_loop(0, slots // PAIR, backward, 0, unroll=2)
+    give_back(1)
+    made[2] = acc_k[lead:, :].astype(jnp.bfloat16).reshape(slots, block_len, head_dim)
+    give_back(2)
+
     for step in range(1, dp_size):
         source_dp = lax.rem(my_dp - step + dp_size, dp_size)
         swap = pltpu.make_async_remote_copy(
@@ -289,7 +289,7 @@
     next_ref[...] = decay_rate * cent_ref[...] + (1.0 - decay_rate) * total
 
     for at, result in enumerate(results):
-        if at > 1:
+        if at > 0:
             wait_sent(at)
         moved = bytes_of(at)
         pltpu.make_async_copy(moved, moved, back_recv.at[at]).wait()
@@ -301,12 +301,18 @@
 
 def settle_kernel(*refs):
     held, results, staged, loaded, stored = refs[:5], refs[5:10], refs[10:15], refs[15], refs[16]
-    loads = [
-        pltpu.make_async_copy(held[at], staged[at], loaded.at[at]) for at in range(5)
-    ]
-    stores = [
-        pltpu.make_async_copy(staged[at], results[at], stored.at[at]) for at in range(5)
-    ]
+    loads, stores = [], []
+    for at in range(5):
+        rows = held[at].shape[0]
+        half = max(1, rows // 2)
+        for cut in range(rows // half):
+            piece = pl.ds(cut * half, half)
+            loads.append(pltpu.make_async_copy(
+                held[at].at[piece], staged[at].at[piece], loaded.at[at, cut]
+            ))
+            stores.append(pltpu.make_async_copy(
+                staged[at].at[piece], results[at].at[piece], stored.at[at, cut]
+            ))
     for load in loads:
         load.start()
     for load, store in zip(loads, stores):
@@ -419,7 +425,7 @@
             in_specs=[any_spec] * 5,
             out_specs=(any_spec,) * 5,
             scratch_shapes=[pltpu.VMEM(item.shape, item.dtype) for item in results]
-            + [pltpu.SemaphoreType.DMA((5,))] * 2,
+            + [pltpu.SemaphoreType.DMA((5, 2))] * 2,
             compiler_params=pltpu.CompilerParams(vmem_limit_bytes=60 * 1024 * 1024),
         )(*results)
     return tuple(unpack(item) for item in results[:4]) + (results[4],)

time: 104 us -> 103 us (level)
  no operation moved by 1% of the time
where the time goes in v5:
time: 103 us
  Pallas kernels  103 us (100%)
    pallas_call x1, Pallas kernels, per_device(): pl.pallas_call(functools.partial(routed_kernel, seq_size, dp_size, slot_c...  100 us
    pallas_call x1, Pallas kernels, per_device(): pl.pallas_call(settle_kernel, out_shape=tuple((jax.ShapeDtypeStruct(item....  2.44 us

profile of v5, /device:TPU:0, one launch (start us, length us, event | category | flops | bytes accessed | tf_op | source)
XLA Modules:
  0.0 103.2 jit_solution(12466034772176205461)
XLA Ops:
  0.6 100.2 %shard_map.101 = (bf16[2,64,2048]{2,1,0:T(8,128)(2,1)}, bf16[2,64,2048]{2,1,0:T(8,128)(2,1)}, bf16[2,64,2048]{2,1,0:T(8,128)(2,1)}, bf16[2,64,2048]{2,1,0:T(8,128)(2,1)}, f32[128,128]{1,0:T(8,128)}) custom-call(s32[4,128]{1,0:T(4,128)} %bitcast.15, f32[128,128]{1,0:T(8,128)} %cent_ref.1, bf16[2,64,2048]{2,1,0:T(8,128)(2,1)} %bitcast.11, ...), custom_call_target="tpu_custom_call" | custom-call | tf_op jit(solution)/shard_map/pallas_call | solution.py:389
  100.8 2.4 %shard_map.102 = (bf16[2,64,2048]{2,1,0:T(8,128)(2,1)}, bf16[2,64,2048]{2,1,0:T(8,128)(2,1)}, bf16[2,64,2048]{2,1,0:T(8,128)(2,1)}, bf16[2,64,2048]{2,1,0:T(8,128)(2,1)}, f32[128,128]{1,0:T(8,128)}) custom-call(bf16[2,64,2048]{2,1,0:T(8,128)(2,1)} %get-tuple-element.15.refs_0_, bf16[2,64,2048]{2,1,0:T(8,128)(2,1)} %get-tuple-element.16.refs_1_, ...), custom_call_target="tpu_custom_call" | custom-call | tf_op jit(solution)/shard_map/pallas_call | solution.py:422

commit v6 on v5

--- a/solution.py
+++ b/solution.py
@@ -55,8 +55,7 @@
     def partner(step):
         if seq_size & (seq_size - 1):
             return lax.rem(me + step, seq_size)
-        odd = lax.rem(step, 2)
-        offset = odd * (seq_size // 2) + step // 2
+        offset = seq_size - step
         target = 0
         for bit in range(seq_size.bit_length() - 1):
             mine = lax.rem(me // (1 << bit), 2)

time: 103 us -> 103 us (level)
  no operation moved by 1% of the time
where the time goes in v6:
time: 103 us
  Pallas kernels  102 us (99%)
    pallas_call x1, Pallas kernels, per_device(): pl.pallas_call(functools.partial(routed_kernel, seq_size, dp_size, slot_c...  99.9 us
    pallas_call x1, Pallas kernels, per_device(): pl.pallas_call(settle_kernel, out_shape=tuple((jax.ShapeDtypeStruct(item....  2.44 us

profile of v6, /device:TPU:0, one launch (start us, length us, event | category | flops | bytes accessed | tf_op | source)
XLA Modules:
  0.0 103.0 jit_solution(626949860686278512)
XLA Ops:
  0.6 99.9 %shard_map.101 = (bf16[2,64,2048]{2,1,0:T(8,128)(2,1)}, bf16[2,64,2048]{2,1,0:T(8,128)(2,1)}, bf16[2,64,2048]{2,1,0:T(8,128)(2,1)}, bf16[2,64,2048]{2,1,0:T(8,128)(2,1)}, f32[128,128]{1,0:T(8,128)}) custom-call(s32[4,128]{1,0:T(4,128)} %bitcast.15, f32[128,128]{1,0:T(8,128)} %cent_ref.1, bf16[2,64,2048]{2,1,0:T(8,128)(2,1)} %bitcast.11, ...), custom_call_target="tpu_custom_call" | custom-call | tf_op jit(solution)/shard_map/pallas_call | solution.py:388
  100.6 2.4 %shard_map.102 = (bf16[2,64,2048]{2,1,0:T(8,128)(2,1)}, bf16[2,64,2048]{2,1,0:T(8,128)(2,1)}, bf16[2,64,2048]{2,1,0:T(8,128)(2,1)}, bf16[2,64,2048]{2,1,0:T(8,128)(2,1)}, f32[128,128]{1,0:T(8,128)}) custom-call(bf16[2,64,2048]{2,1,0:T(8,128)(2,1)} %get-tuple-element.15.refs_0_, bf16[2,64,2048]{2,1,0:T(8,128)(2,1)} %get-tuple-element.16.refs_1_, ...), custom_call_target="tpu_custom_call" | custom-call | tf_op jit(solution)/shard_map/pallas_call | solution.py:421
